TPU v7x, 512 devices: a whole 4x8x8 slice. The times are simulated.
512 devices in a mesh: blk: 64 (over y, x, core), tp: 8 (over z).
Axes of the slice: x: 4, y: 8, z: 8, core: 2. Of those that a mesh axis runs over, the one named last changes fastest.
Arguments:
- inputs: bfloat16 [8192, 8192], P('blk', 'tp'), may hold values from -6 to 6
- grad_out: bfloat16 [8192, 8192], P('blk', 'tp'), may hold values from -6 to 6
- w_up: bfloat16 [128, 2, 128, 128], P('blk'), may hold values from -0.4375 to 0.4375
- w_down: bfloat16 [128, 2, 128, 128], P('blk'), may hold values from -0.3125 to 0.3125
- up_rows: int32 [128, 2], P('blk'), may hold values from 0 to 63, as said below
- slot_counts: int32 [128], P('blk'), may hold values from 1 to 2
- keep_mask: int32 [8192, 1024], P(None, 'blk'), may hold values from 0 to 65535, as said below
Outputs:
- outputs: bfloat16 [8192, 8192], P('blk', 'tp')
- grad_in: bfloat16 [8192, 8192], P('blk', 'tp')
- grad_up: bfloat16 [128, 2, 128, 128], P('blk', None, 'tp')
- grad_down: bfloat16 [128, 2, 128, 128], P('blk', None, 'tp')
Inputs may be any that keep to these rules, and one draw needn't show every extreme that they name: `up_rows`: within each hidden column block, the 2 entries are distinct. `keep_mask`: bit k of word w holds the keep flag of hidden unit 16 w + k.
All inputs are finite; a program needn't handle non-finite values.
Results may differ from a plain program's by a relative error of at most 0.005.
Values may be sent and summed in bfloat16 or wider, within the bound.
A program may use at most 64 MiB of HBM per device.

v0:
```python
import jax
import jax.numpy as jnp
from jax import lax
from jax.sharding import PartitionSpec as P

INV_ROOT_TWO = 0.7071067811865476
INV_ROOT_TAU = 0.3989422804014327
KEEP_SCALE = 1.25


def gelu_value(value):
    return 0.5 * value * (1.0 + jax.scipy.special.erf(value * INV_ROOT_TWO))


def gelu_slope(value):
    return (
        0.5 * (1.0 + jax.scipy.special.erf(value * INV_ROOT_TWO))
        + value * jnp.exp(-0.5 * value * value) * INV_ROOT_TAU
    )


def combine_terms(received, flat_owner, part_rows, row_blocks, tile):
    selector = (flat_owner[:, None] == jnp.arange(row_blocks, dtype=jnp.int32)[None, :]).astype(
        jnp.float32
    )
    stacked = received.reshape(part_rows, flat_owner.shape[0], tile)
    summed = jnp.einsum("nsl,sr->nrl", stacked, selector, precision=lax.Precision.HIGHEST)
    return summed.reshape(part_rows, row_blocks * tile).astype(jnp.bfloat16)


def per_device(inputs, grad_out, w_up, w_down, up_rows, slot_counts, keep_mask):
    tok_dev, width_local = inputs.shape
    col_local, slots, tile, _unused = w_up.shape
    parts = lax.axis_size("tp")
    blocks = lax.axis_size("blk")
    width = width_local * parts
    row_blocks = width // tile
    part_rows = tok_dev // parts
    held = part_rows * blocks
    span = col_local * slots
    live = jnp.arange(slots, dtype=jnp.int32)[None, :] < slot_counts[:, None]
    live_tiles = live[:, :, None, None]
    up_live = jnp.where(live_tiles, w_up, jnp.zeros((), jnp.bfloat16))
    down_live = jnp.where(live_tiles, w_down, jnp.zeros((), jnp.bfloat16))
    owner_rows = lax.all_gather(up_rows, "blk", axis=0, tiled=True)
    flat_owner = owner_rows.reshape(-1)

    def select_tiles(rows_full):
        blocked = rows_full.reshape(part_rows, row_blocks, tile)
        return jnp.take(blocked, flat_owner, axis=1).reshape(part_rows, blocks, span * tile)

    def as_tiles(received):
        return received.reshape(held, col_local, slots, tile)

    def combine(received):
        return combine_terms(received, flat_owner, part_rows, row_blocks, tile)

    in_rows, out_rows = (
        lax.all_to_all(inputs, "tp", split_axis=0, concat_axis=1, tiled=True),
        lax.all_to_all(grad_out, "tp", split_axis=0, concat_axis=1, tiled=True),
    )
    recv_in, recv_out = (
        lax.all_to_all(select_tiles(in_rows), "blk", split_axis=1, concat_axis=0, tiled=True),
        lax.all_to_all(select_tiles(out_rows), "blk", split_axis=1, concat_axis=0, tiled=True),
    )
    input_tiles = as_tiles(recv_in)
    cotangent_tiles = as_tiles(recv_out)
    word_count = keep_mask.shape[1]
    words = keep_mask.reshape(blocks, parts, part_rows, word_count)
    mine = lax.dynamic_index_in_dim(words, lax.axis_index("tp"), 1, keepdims=False).reshape(
        held, word_count
    )
    columns = jnp.arange(col_local * tile, dtype=jnp.int32)
    picked = jnp.take(mine, columns // 16, axis=1)
    keep = jnp.bitwise_and(jnp.right_shift(picked, columns % 16), 1)
    scale = keep.astype(jnp.float32) * KEEP_SCALE
    pre = jnp.einsum(
        "nckp,ckpj->ncj", input_tiles, up_live, preferred_element_type=jnp.float32
    ).reshape(held, col_local * tile)
    hidden = (gelu_value(pre) * scale).astype(jnp.bfloat16)
    hidden_blocks = hidden.reshape(held, col_local, tile)
    out_part = jnp.einsum(
        "ncj,ckjl->nckl", hidden_blocks, down_live, preferred_element_type=jnp.float32
    ).reshape(held, span * tile)
    out_recv = lax.all_to_all(out_part, "blk", split_axis=0, concat_axis=1, tiled=True)
    outputs = lax.all_to_all(combine(out_recv), "tp", split_axis=1, concat_axis=0, tiled=True)
    grad_hidden = jnp.einsum(
        "nckl,ckjl->ncj", cotangent_tiles, down_live, preferred_element_type=jnp.float32
    ).reshape(held, col_local * tile)
    grad_pre = (grad_hidden * scale * gelu_slope(pre)).astype(jnp.bfloat16)
    grad_blocks = grad_pre.reshape(held, col_local, tile)
    in_part = jnp.einsum(
        "ncj,ckpj->nckp", grad_blocks, up_live, preferred_element_type=jnp.float32
    ).reshape(held, span * tile)
    in_recv = lax.all_to_all(in_part, "blk", split_axis=0, concat_axis=1, tiled=True)
    grad_in = lax.all_to_all(combine(in_recv), "tp", split_axis=1, concat_axis=0, tiled=True)
    up_sum = jnp.einsum(
        "nckp,ncj->ckpj", input_tiles, grad_blocks, preferred_element_type=jnp.float32
    )
    down_sum = jnp.einsum(
        "ncj,nckl->ckjl", hidden_blocks, cotangent_tiles, preferred_element_type=jnp.float32
    )
    up_share, down_share = (
        lax.psum_scatter(up_sum, "tp", scatter_dimension=2, tiled=True),
        lax.psum_scatter(down_sum, "tp", scatter_dimension=2, tiled=True),
    )
    grad_up = jnp.where(live_tiles, up_share, 0.0).astype(jnp.bfloat16)
    grad_down = jnp.where(live_tiles, down_share, 0.0).astype(jnp.bfloat16)
    return (outputs, grad_in, grad_up, grad_down)


def solution(mesh):
    return jax.shard_map(
        per_device,
        mesh=mesh,
        in_specs=(
            P("blk", "tp"),
            P("blk", "tp"),
            P("blk", None, None, None),
            P("blk", None, None, None),
            P("blk", None),
            P("blk"),
            P(None, "blk"),
        ),
        out_specs=(
            P("blk", "tp"),
            P("blk", "tp"),
            P("blk", None, "tp", None),
            P("blk", None, "tp", None),
        ),
        check_vma=False,
    )
```

profile of v0, /device:TPU:6, one launch (start us, length us, event | category | flops | bytes accessed | tf_op | source)
XLA Modules:
  0.0 339.3 jit_solution(14502978726614844054)
XLA Ops:
  7.2 10.3 %all-to-all-start = ((bf16[8,16,1024]{2,1,0:T(8,128)(2,1)}), bf16[8,16,1024]{2,1,0:T(8,128)(2,1)S(1)}, u32[]{:S(2)}, u32[]{:S(2)}) async-start(bf16[8,16,1024]{2,1,0:T(8,128)(2,1)} %bitcast.100), calls=%async_computation | async-start | bytes 524288 | tf_op jit(solution)/shard_map/all_to_all | solution.py:59
  17.5 38.4 %all-gather = s32[64,2,2]{2,1,0:T(2,128)S(1)} all-gather(s32[1,2,2]{2,1,0:T(2,128)} %bitcast.102), channel_id=1, replica_groups=mesh['blk'=64,'tp'=8] {'blk'}, dimensions={0}, use_global_device_ids=true | all-gather | bytes 1040 | tf_op jit(solution)/shard_map/all_gather | solution.py:45
  56.0 7.2 %all-to-all-start.4 = ((bf16[8,16,1024]{2,1,0:T(8,128)(2,1)}), bf16[8,16,1024]{2,1,0:T(8,128)(2,1)S(1)}, u32[]{:S(2)}, u32[]{:S(2)}) async-start(bf16[8,16,1024]{2,1,0:T(8,128)(2,1)} %bitcast.101), calls=%async_computation.4 | async-start | bytes 524288 | tf_op jit(solution)/shard_map/all_to_all | solution.py:60
  63.3 0.2 copy.50
  63.5 0.2 copy.51
  63.7 12.1 %all-to-all-done.4 = bf16[8,16,1024]{2,1,0:T(8,128)(2,1)S(1)} async-done(((bf16[8,16,1024]{2,1,0:T(8,128)(2,1)}), bf16[8,16,1024]{2,1,0:T(8,128)(2,1)S(1)}, u32[]{:S(2)}, u32[]{:S(2)}) %all-to-all-start.4) | async-done | bytes 262176 | tf_op jit(solution)/shard_map/all_to_all | solution.py:60
  75.8 0.1 copy.61
  76.1 0.2 copy.62
  76.3 0.8 gather_fusion.1
  77.1 0.8 gather_fusion.2
  78.0 0.9 select_bitcast_fusion
  78.9 0.3 copy.52
  79.2 0.7 reshape.186
  79.9 1.6 copy.53
  81.5 8.4 %all-to-all-start.1 = ((bf16[16,64,512]{2,0,1:T(8,128)(2,1)}), bf16[16,64,512]{2,0,1:T(8,128)(2,1)S(1)}, u32[]{:S(2)}, u32[]{:S(2)}) async-start(bf16[16,64,512]{2,0,1:T(8,128)(2,1)} %copy.53), calls=%async_computation.1 | async-start | bytes 2097152 | tf_op jit(solution)/shard_map/all_to_all | solution.py:63
  89.8 0.3 copy.63
  90.1 0.7 reshape.192
  90.8 1.5 copy.64
  92.3 26.3 %all-to-all-done.1 = bf16[16,64,512]{2,0,1:T(8,128)(2,1)S(1)} async-done(((bf16[16,64,512]{2,0,1:T(8,128)(2,1)}), bf16[16,64,512]{2,0,1:T(8,128)(2,1)S(1)}, u32[]{:S(2)}, u32[]{:S(2)}) %all-to-all-start.1) | async-done | bytes 1048608 | tf_op jit(solution)/shard_map/all_to_all | solution.py:63
  118.7 5.8 %all-to-all-start.5 = ((bf16[16,64,512]{2,0,1:T(8,128)(2,1)}), bf16[16,64,512]{2,0,1:T(8,128)(2,1)}, u32[]{:S(2)}, u32[]{:S(2)}) async-start(bf16[16,64,512]{2,0,1:T(8,128)(2,1)} %copy.64), calls=%async_computation.5 | async-start | bytes 2097152 | tf_op jit(solution)/shard_map/all_to_all | solution.py:64
  124.5 2.8 reshape.188
  127.3 3.7 %dynamic-slice_reduce_fusion = s32[64,16,16]{1,0,2:T(8,128)S(1)} fusion(s32[64,8,16,16]{2,1,0,3:T(8,128)} %reshape.188, s32[]{:T(128)S(6)} %select_n.78), kind=kLoop, calls=%fused_computation.27 | loop fusion | bytes 131076 | tf_op jit(solution)/shard_map/jit(dynamic_index_in_dim)/dynamic_slice | solution.py:70
  131.0 0.3 reshape.189
  131.3 1.1 gather_fusion
  132.5 1.2 reshape.187
  133.7 2.4 copy.70
  136.2 17.0 %all-to-all-done.5 = bf16[16,64,512]{2,0,1:T(8,128)(2,1)} async-done(((bf16[16,64,512]{2,0,1:T(8,128)(2,1)}), bf16[16,64,512]{2,0,1:T(8,128)(2,1)}, u32[]{:S(2)}, u32[]{:S(2)}) %all-to-all-start.5) | async-done | bytes 1048608 | tf_op jit(solution)/shard_map/all_to_all | solution.py:64
  153.2 2.2 reshape.193
  155.4 3.7 %copy.72 = bf16[1024,2,2,128]{0,3,2,1:T(8,128)(2,1)} copy(bf16[1024,2,2,128]{3,2,1,0:T(2,128)(2,1)} %reshape.193) | data formatting | bytes 2097152 | tf_op jit(solution)/shard_map/reshape | solution.py:53
  159.1 0.4 convolution_bitcast_fusion.3
  159.6 0.8 copy-done.4
  160.4 0.8 fusion.3
  161.2 0.9 copy-done.6
  162.1 1.8 convolution_bitcast_fusion
  163.9 3.1 copy.67
  167.0 2.7 all_to_all.112
  169.7 5.6 %all-to-all-start.6 = ((f32[64,16,512]{2,1,0:T(8,128)}), f32[64,16,512]{2,1,0:T(8,128)S(1)}, u32[]{:S(2)}, u32[]{:S(2)}) async-start(f32[64,16,512]{2,1,0:T(8,128)} %all_to_all.112), calls=%async_computation.6 | async-start | bytes 4194304 | tf_op jit(solution)/shard_map/all_to_all | solution.py:95
  175.3 2.0 fusion.10
  177.3 0.8 copy-done.1
  178.1 1.9 convolution_bitcast_fusion.1
  179.9 4.1 %copy.58 = f32[1024,2,2,128]{3,2,1,0:T(2,128)} copy(f32[1024,2,2,128]{0,3,2,1:T(8,128)} %convolution_bitcast_fusion.1) | data formatting | bytes 4194304 | tf_op jit(solution)/shard_map/ncj,ckjl->nckl/transpose | solution.py:82
  184.1 3.9 %all_to_all.100 = f32[64,16,512]{2,1,0:T(8,128)} reshape(f32[1024,2,2,128]{3,2,1,0:T(2,128)} %copy.58) | data formatting | bytes 4194304 | tf_op jit(solution)/shard_map/all_to_all | solution.py:85
  187.9 38.6 %all-to-all-done.6 = f32[64,16,512]{2,1,0:T(8,128)S(1)} async-done(((f32[64,16,512]{2,1,0:T(8,128)}), f32[64,16,512]{2,1,0:T(8,128)S(1)}, u32[]{:S(2)}, u32[]{:S(2)}) %all-to-all-start.6) | async-done | bytes 2097184 | tf_op jit(solution)/shard_map/all_to_all | solution.py:95
  226.6 1.3 copy-done
  227.9 5.4 %all-to-all-start.2 = ((f32[64,16,512]{2,1,0:T(8,128)}), f32[64,16,512]{2,1,0:T(8,128)S(1)}, u32[]{:S(2)}, u32[]{:S(2)}) async-start(f32[64,16,512]{2,1,0:T(8,128)} %all_to_all.100), calls=%async_computation.2 | async-start | bytes 4194304 | tf_op jit(solution)/shard_map/all_to_all | solution.py:85
  233.3 0.3 reduce-scatter.3.cloned.1.call-start
  233.6 2.2 fusion.26
  235.8 4.2 %copy.68 = f32[16,64,512]{2,1,0:T(8,128)} copy(f32[16,64,512]{2,0,1:T(8,128)} %bitcast.92) | data formatting | bytes 4194304 | tf_op jit(solution)/shard_map/all_to_all | solution.py:95
  239.9 2.6 reshape.194
  242.5 2.6 fusion.5
  245.2 0.9 copy.69
  246.1 38.5 %all-to-all-done.2 = f32[64,16,512]{2,1,0:T(8,128)S(1)} async-done(((f32[64,16,512]{2,1,0:T(8,128)}), f32[64,16,512]{2,1,0:T(8,128)S(1)}, u32[]{:S(2)}, u32[]{:S(2)}) %all-to-all-start.2) | async-done | bytes 2097184 | tf_op jit(solution)/shard_map/all_to_all | solution.py:85
  284.6 3.4 %all-to-all-start.7 = ((bf16[16,8,1024]{2,0,1:T(8,128)(2,1)}), bf16[16,8,1024]{2,0,1:T(8,128)(2,1)S(1)}, u32[]{:S(2)}, u32[]{:S(2)}) async-start(bf16[16,8,1024]{2,0,1:T(8,128)(2,1)} %copy.69), calls=%async_computation.7 | async-start | bytes 524288 | tf_op jit(solution)/shard_map/all_to_all | solution.py:96
  288.1 2.4 convolution_bitcast_fusion.4
  290.5 2.5 copy.59
  293.1 1.6 reshape.190
  294.7 0.9 fusion.4
  295.7 0.9 copy.60
  296.6 2.2 all-to-all-done.7
  298.8 4.9 %all-to-all-start.3 = ((bf16[16,8,1024]{2,0,1:T(8,128)(2,1)}), bf16[16,8,1024]{2,0,1:T(8,128)(2,1)S(1)}, u32[]{:S(2)}, u32[]{:S(2)}) async-start(bf16[16,8,1024]{2,0,1:T(8,128)(2,1)} %copy.60), calls=%async_computation.3 | async-start | bytes 524288 | tf_op jit(solution)/shard_map/all_to_all | solution.py:86
  303.7 25.8 %reduce-scatter.5.cloned.1.call-done = f32[2,2,16,128]{3,2,1,0:T(8,128)} async-done(((f32[2,2,128,128]{3,2,1,0:T(8,128)}), f32[2,2,16,128]{3,2,1,0:T(8,128)}) %reduce-scatter.5.cloned.1.call-update) | async-done | bytes 32784 | tf_op jit(solution)/shard_map/reduce_scatter | solution.py:105
  329.5 1.5 select_convert_fusion
  331.0 0.7 copy.94
  331.7 0.7 copy.95
  (37 shorter events, 0.9 us)
Async XLA Ops:
  7.2 48.8 %all-to-all-start = ((bf16[8,16,1024]{2,1,0:T(8,128)(2,1)}), bf16[8,16,1024]{2,1,0:T(8,128)(2,1)S(1)}, u32[]{:S(2)}, u32[]{:S(2)}) async-start(bf16[8,16,1024]{2,1,0:T(8,128)(2,1)} %bitcast.100), calls=%async_computation | async-start | bytes 524288 | tf_op jit(solution)/shard_map/all_to_all | solution.py:59
  56.0 19.8 %all-to-all-start.4 = ((bf16[8,16,1024]{2,1,0:T(8,128)(2,1)}), bf16[8,16,1024]{2,1,0:T(8,128)(2,1)S(1)}, u32[]{:S(2)}, u32[]{:S(2)}) async-start(bf16[8,16,1024]{2,1,0:T(8,128)(2,1)} %bitcast.101), calls=%async_computation.4 | async-start | bytes 524288 | tf_op jit(solution)/shard_map/all_to_all | solution.py:60
  81.5 37.2 %all-to-all-start.1 = ((bf16[16,64,512]{2,0,1:T(8,128)(2,1)}), bf16[16,64,512]{2,0,1:T(8,128)(2,1)S(1)}, u32[]{:S(2)}, u32[]{:S(2)}) async-start(bf16[16,64,512]{2,0,1:T(8,128)(2,1)} %copy.53), calls=%async_computation.1 | async-start | bytes 2097152 | tf_op jit(solution)/shard_map/all_to_all | solution.py:63
  90.8 33.7 %copy-start.7 = (s32[8192,16]{0,1:T(8,128)S(1)}, s32[8192,16]{0,1:T(8,128)}, u32[]{:S(2)}) copy-start(s32[8192,16]{0,1:T(8,128)} %param.15) | copy-start | bytes 1572868
  118.7 34.6 %all-to-all-start.5 = ((bf16[16,64,512]{2,0,1:T(8,128)(2,1)}), bf16[16,64,512]{2,0,1:T(8,128)(2,1)}, u32[]{:S(2)}, u32[]{:S(2)}) async-start(bf16[16,64,512]{2,0,1:T(8,128)(2,1)} %copy.64), calls=%async_computation.5 | async-start | bytes 2097152 | tf_op jit(solution)/shard_map/all_to_all | solution.py:64
  131.3 1.1 copy-start.10
  132.4 27.2 %copy-start.3 = (s32[256,1024]{1,0:T(8,128)}, s32[256,1024]{1,0:T(8,128)S(1)}, u32[]{:S(2)}) copy-start(s32[256,1024]{1,0:T(8,128)S(1)} %gather_fusion) | copy-start | bytes 3145732
  153.2 5.9 %copy-start.8 = (bf16[2,2,128,128]{3,2,1,0:T(8,128)(2,1)S(1)}, bf16[2,2,128,128]{3,2,1,0:T(8,128)(2,1)}, u32[]{:S(2)}) copy-start(bf16[2,2,128,128]{3,2,1,0:T(8,128)(2,1)} %param.11) | copy-start | bytes 393220
  155.4 4.1 %copy-start.9 = (bf16[2,2,128,128]{3,2,1,0:T(8,128)(2,1)S(1)}, bf16[2,2,128,128]{3,2,1,0:T(8,128)(2,1)}, u32[]{:S(2)}) copy-start(bf16[2,2,128,128]{3,2,1,0:T(8,128)(2,1)} %param.12) | copy-start | bytes 393220
  159.1 1.2 copy-start.4
  159.6 1.6 copy-start.5
  161.2 0.9 copy-start.6
  169.7 56.9 %all-to-all-start.6 = ((f32[64,16,512]{2,1,0:T(8,128)}), f32[64,16,512]{2,1,0:T(8,128)S(1)}, u32[]{:S(2)}, u32[]{:S(2)}) async-start(f32[64,16,512]{2,1,0:T(8,128)} %all_to_all.112), calls=%async_computation.6 | async-start | bytes 4194304 | tf_op jit(solution)/shard_map/all_to_all | solution.py:95
  177.3 0.8 copy-start.1
  226.6 1.3 copy-start
  227.9 56.7 %all-to-all-start.2 = ((f32[64,16,512]{2,1,0:T(8,128)}), f32[64,16,512]{2,1,0:T(8,128)S(1)}, u32[]{:S(2)}, u32[]{:S(2)}) async-start(f32[64,16,512]{2,1,0:T(8,128)} %all_to_all.100), calls=%async_computation.2 | async-start | bytes 4194304 | tf_op jit(solution)/shard_map/all_to_all | solution.py:85
  233.3 70.4 %reduce-scatter.3.cloned.1.call-start = ((), (), s32[]{:S(2)}) async-start(), calls=%async_computation.10 | async-start | bytes 294912 | tf_op jit(solution)/shard_map/reduce_scatter | solution.py:104
  242.5 45.5 %copy-start.2 = (bf16[1024,2,128,1]{0,2,3,1:T(8,128)(2,1)S(1)}, bf16[1024,2,128,1]{0,2,3,1:T(8,128)(2,1)}, u32[]{:S(2)}) copy-start(bf16[1024,2,128,1]{0,2,3,1:T(8,128)(2,1)} %copy-done.1) | copy-start | bytes 1572868
  284.6 14.2 %all-to-all-start.7 = ((bf16[16,8,1024]{2,0,1:T(8,128)(2,1)}), bf16[16,8,1024]{2,0,1:T(8,128)(2,1)S(1)}, u32[]{:S(2)}, u32[]{:S(2)}) async-start(bf16[16,8,1024]{2,0,1:T(8,128)(2,1)} %copy.69), calls=%async_computation.7 | async-start | bytes 524288 | tf_op jit(solution)/shard_map/all_to_all | solution.py:96
  288.0 41.5 %reduce-scatter.5.cloned.1.call-start = ((), (), s32[]{:S(2)}) async-start(), calls=%async_computation.11 | async-start | bytes 294912 | tf_op jit(solution)/shard_map/reduce_scatter | solution.py:105
  298.8 32.3 %all-to-all-start.3 = ((bf16[16,8,1024]{2,0,1:T(8,128)(2,1)}), bf16[16,8,1024]{2,0,1:T(8,128)(2,1)S(1)}, u32[]{:S(2)}, u32[]{:S(2)}) async-start(bf16[16,8,1024]{2,0,1:T(8,128)(2,1)} %copy.60), calls=%async_computation.3 | async-start | bytes 524288 | tf_op jit(solution)/shard_map/all_to_all | solution.py:86
Sparse Core Ops, SparseCore 0:
  236.9 35.9 reduce-scatter.2
  291.9 37.6 reduce-scatter.4
where the time goes:
time: 341 us; the launch traced here: 339 us
  waiting for transfers between devices  161 us (47%)
  local copies, waits for them, and re-layouts  56.9 us (17%)
  starting transfers between devices  51.4 us (15%)
  blocking collectives  38.4 us (11%)
  between operations  14.4 us (4%)
  matrix products  13 us (4%)
  other arithmetic  4.48 us (1%)
    all_to_all x1, waiting for transfers between devices, per_device(): lax.all_to_all(in_part, 'blk', split_axis=0, concat_axis=1, tiled=True)  38.6 us
    all_to_all x1, waiting for transfers between devices, per_device(): lax.all_to_all(out_part, 'blk', split_axis=0, concat_axis=1, tiled=True)  38.5 us
    all_gather x1, blocking collectives, per_device(): owner_rows = lax.all_gather(up_rows, 'blk', axis=0, tiled=True)  38.4 us
    all_to_all x1, waiting for transfers between devices, per_device(): lax.all_to_all(select_tiles(in_rows), 'blk', split_axis=1, concat_axis=0,...  26.3 us
    reduce_scatter x1, waiting for transfers between devices, per_device(): lax.psum_scatter(down_sum, 'tp', scatter_dimension=2, tiled=True)  25.8 us
    all_to_all x1, waiting for transfers between devices, per_device(): lax.all_to_all(select_tiles(out_rows), 'blk', split_axis=1, concat_axis=0...  17 us
    all_to_all x1, waiting for transfers between devices, per_device(): lax.all_to_all(grad_out, 'tp', split_axis=0, concat_axis=1, tiled=True)  12.1 us
    all_to_all x1, starting transfers between devices, per_device(): lax.all_to_all(inputs, 'tp', split_axis=0, concat_axis=1, tiled=True)  10.3 us
  transfers between devices with their start and end apart: 10, of which 7 were waited for; matrix products, arithmetic and copies ran while one was open for 13% of the time, Pallas kernels for 0%

commit v1 on v0

v1 whole, which is shorter than its diff:
```python
import functools

import jax
import jax.numpy as jnp
from jax import lax
from jax.experimental import pallas as pl
from jax.experimental.pallas import tpu as pltpu
from jax.sharding import PartitionSpec as P

INV_ROOT_TWO = 0.7071067811865476
INV_ROOT_TAU = 0.3989422804014327
KEEP_SCALE = 1.25
MESH = pl.DeviceIdType.MESH
X_CHIPS = 4
BF = jnp.bfloat16
F32 = jnp.float32
I32 = jnp.int32


def dot(a, b, ca, cb):
    return lax.dot_general(a, b, (((ca,), (cb,)), ((), ())), preferred_element_type=F32)


def iota(shape, dim):
    return lax.broadcasted_iota(I32, shape, dim)


def kernel(
    dims,
    x_ref, dy_ref, wu_ref, wd_ref, keep_ref, rows_ref, cnt_ref,
    out_ref, gin_ref, gup_ref, gdn_ref,
    zst, full_x, full_dy, rows_a, rows_b, rows_s, wu, wd, tokw, maskw, mask_st, scale,
    tile_st, tile_in, slope, hid, gpre, term_st, term_in, lanes, hot,
    zo_st, zo_in, gst, gin_z, gsum, gpart,
    z_send, z_recv, a_send, a_recv, b_send, b_recv, p_send, p_recv,
    d_send, d_recv, t_send, t_recv, o_send, o_recv, g_send, g_recv, l_sem,
):
    YN, XN, ZN, PT, RL = dims
    XC = XN * 2
    HALF = YN // 2
    LO = HALF // 2 - 1
    ND = HALF * XC
    RB = RL * ZN
    GT = XC * PT
    blk, z = lax.axis_index("blk"), lax.axis_index("tp")
    c = lax.rem(blk, 2)
    x = lax.rem(blk // 2, XN)
    y = blk // XC
    xc = x * 2 + c
    up = jnp.where(y >= HALF, 1, 0)
    partner = lax.rem(y + HALF, YN) * XC + xc

    def mod(v, n):
        return lax.rem(v + n, n)

    def remote(src, dst, ss, rs, b, t):
        return pltpu.make_async_remote_copy(
            src_ref=src, dst_ref=dst, send_sem=ss, recv_sem=rs, device_id=(b, t), device_id_type=MESH
        )

    barrier = pltpu.get_barrier_semaphore()
    peers = []
    for dy in range(-(HALF // 2), YN - HALF // 2):
        for xo in range(XN):
            for co in range(2):
                if (dy, xo, co) == (0, 0, 0):
                    continue
                if abs(dy) <= HALF // 2 or (xo, co) == (0, 0):
                    peers.append((mod(y + dy, YN) * XC + lax.rem(x + xo, XN) * 2 + lax.rem(c + co, 2), z))
    for zo in range(1, ZN):
        peers.append((blk, lax.rem(z + zo, ZN)))
    for b, t in peers:
        pl.semaphore_signal(barrier, inc=1, device_id=(b, t), device_id_type=MESH)

    full = (full_x, full_dy)
    lane = iota((8, 128), 1)
    mine = jnp.where(lane == 0, rows_ref[0, 0], jnp.where(lane == 1, rows_ref[0, 1],
                     jnp.where(lane == 2, rows_ref[1, 0], rows_ref[1, 1])))
    rows_a[xc] = mine
    for a, ref in enumerate((x_ref, dy_ref)):
        for t in range(ZN):
            for i in range(RL):
                zst[a, t, i] = ref[t * PT:(t + 1) * PT, i * 128:(i + 1) * 128]
        full[a][pl.ds(z * RL, RL)] = zst[a, z]
    for cl in range(2):
        for s in range(2):
            live = s < cnt_ref[cl]
            wu[2 * up + cl, s * 128:(s + 1) * 128, :] = jnp.where(live, wu_ref[cl, s], jnp.zeros((), BF))
            wd[2 * up + cl, :, s * 128:(s + 1) * 128] = jnp.where(live, wd_ref[cl, s], jnp.zeros((), BF))
    pl.semaphore_wait(barrier, len(peers))

    def row_a(o):
        q = lax.rem(xc + o, XC)
        return remote(rows_a.at[xc], rows_a.at[xc], a_send.at[o], a_recv.at[xc], y * XC + q, z)

    for o in range(1, XC):
        row_a(o).start()

    order = [o for k in range(1, ZN // 2 + 1) for o in dict.fromkeys((k, ZN - k))]

    def z_copy(a, o):
        t = lax.rem(z + o, ZN)
        return remote(zst.at[a, t], full[a].at[pl.ds(z * RL, RL)], z_send.at[a, o], z_recv.at[a, z], blk, t)

    for a in range(2):
        for o in order:
            z_copy(a, o).start()
    w_copies = [
        remote(w.at[pl.ds(2 * up, 2)], w.at[pl.ds(2 * up, 2)], p_send.at[k], p_recv.at[k], partner, z)
        for k, w in enumerate((wu, wd))
    ]
    for w_copy in w_copies:
        w_copy.start()

    span = XC * ZN * PT
    r, l = iota((span, GT), 0), iota((span, GT), 1)
    share = ZN * PT
    pick = jnp.where((r // share == l // PT) & (lax.rem(r, share) == z * PT + lax.rem(l, PT)), 1.0, 0.0).astype(BF)
    for g in range(YN):
        words = keep_ref[:, g * span:(g + 1) * span]
        low = jnp.bitwise_and(words, 255).astype(F32).astype(BF)
        high = jnp.right_shift(words, 8).astype(F32).astype(BF)
        found = dot(jnp.concatenate([low, high], axis=0), pick, 1, 0).astype(I32)
        tokw[g] = found[:16] + found[16:] * 256
    for j in range(HALF):
        maskw[up, j] = tokw[mod(y + j - LO - c, YN)]
        mask_st[j] = tokw[lax.rem(y + HALF + j - LO - c + YN, YN)]
    m_copy = remote(mask_st, maskw.at[up], p_send.at[2], p_recv.at[2], partner, z)
    m_copy.start()

    def wait_a(o):
        q = lax.rem(xc + o, XC)
        remote(rows_a.at[q], rows_a.at[q], a_send.at[o], a_recv.at[q], blk, z).wait_recv()

    for o in range(1, XC):
        wait_a(o)
    sub = iota((8, 128), 0)
    packed = rows_a[0]
    for q in range(1, XC):
        packed = jnp.where(sub == q, rows_a[q], packed)
    rows_b[y] = packed

    def row_b(o):
        q = lax.rem(y + o, YN)
        return remote(rows_b.at[y], rows_b.at[y], b_send.at[o], b_recv.at[y], q * XC + xc, z)

    for o in range(1, YN):
        row_b(o).start()
    for o in range(1, YN):
        q = lax.rem(y + o, YN)
        remote(rows_b.at[q], rows_b.at[q], b_send.at[o], b_recv.at[q], blk, z).wait_recv()
    to_scalar = pltpu.make_async_copy(rows_b, rows_s, l_sem)
    to_scalar.start()
    to_scalar.wait()

    def label(i):
        j = lax.rem(i, HALF)
        xo = lax.rem(i // HALF, XN)
        co = i // (HALF * XN)
        xd, cd = lax.rem(x + xo, XN), lax.rem(c + co, 2)
        return j, xd, cd, j * XC + xd * 2 + cd

    def token_side(i):
        j, xd, cd, d = label(i)
        yd = lax.rem(y - (j - LO - cd) + YN, YN)
        return d, yd, xd, cd, (yd == y) & (xd == x) & (cd == c), j * XC + xc

    def owner_side(i):
        j, xd, cd, d = label(i)
        yd = lax.rem(y + (j - LO - c) + YN, YN)
        return d, yd, xd, cd, (yd == y) & (xd == x) & (cd == c), j * XC + xc

    def tile_copy(a, i):
        d, yd, xd, cd, own, at = token_side(i)
        return own, lambda: remote(
            tile_st.at[a, d], tile_in.at[a, at], d_send.at[a, d], d_recv.at[a, at], yd * XC + xd * 2 + cd, z
        ), lambda: pltpu.make_async_copy(tile_st.at[a, d], tile_in.at[a, at], d_recv.at[a, at])

    def dispatch(a):
        for o in order:
            s = lax.rem(z + o, ZN)
            remote(zst.at[a, s], full[a].at[pl.ds(s * RL, RL)], z_send.at[a, o], z_recv.at[a, s], blk, z).wait_recv()

        @pl.loop(0, ND)
        def _(i):
            d, yd, xd, cd, own, at = token_side(i)
            low = lax.rem(yd, HALF)
            for k in range(8):
                row = rows_s[low + HALF * (k // 4), xd * 2 + cd, k % 4]
                tile_st[a, d, k] = full[a][row]
            own, far, near = tile_copy(a, i)

            @pl.when(own)
            def _():
                near().start()

            @pl.when(jnp.logical_not(own))
            def _():
                far().start()

    dispatch(0)
    dispatch(1)

    @pl.loop(0, ND)
    def _(i):
        d, yd, xd, cd, own, at = token_side(i)
        low = lax.rem(yd, HALF)
        value = jnp.zeros((8, 128), I32)
        for k in range(8):
            row = rows_s[low + HALF * (k // 4), xd * 2 + cd, k % 4]
            value = jnp.where(lane // PT == k, row * PT, value)
        lanes[d] = value + lax.rem(lane, PT)

    @pl.loop(0, ND)
    def _(d):
        want = lanes[d][0:1, :]
        at = pl.ds(pl.multiple_of(d * 128, 128), 128)
        hot[:, at] = jnp.where(iota((RB * PT, 128), 0) == want, 1.0, 0.0).astype(BF)

    m_wait = remote(mask_st, maskw.at[1 - up], p_send.at[2], p_recv.at[2], partner, z)
    m_wait.wait_recv()
    er, el = iota((32, 256), 0), iota((32, 256), 1)
    spread = jnp.where((el // 16 == lax.rem(er, 16)) & ((lax.rem(el, 16) >= 8) == (er >= 16)), 1.0, 0.0).astype(BF)
    shift = lax.rem(iota((GT, 256), 1), 8)
    for h in range(2):
        for j in range(HALF):
            words = maskw[h, j]
            low = jnp.bitwise_and(words, 255).astype(F32).astype(BF)
            high = jnp.right_shift(words, 8).astype(F32).astype(BF)
            found = dot(jnp.concatenate([low, high], axis=0), spread, 0, 0).astype(I32)
            keep = jnp.bitwise_and(jnp.right_shift(found, shift), 1)
            scale[h, j * GT:(j + 1) * GT, :] = keep.astype(F32) * KEEP_SCALE
    for k, w in enumerate((wu, wd)):
        there = w.at[pl.ds(2 * (1 - up), 2)]
        remote(there, there, p_send.at[k], p_recv.at[k], partner, z).wait_recv()

    def wide(a, col, start, count):
        parts = [tile_in[a, pl.ds(start, count), 2 * col + s].reshape(count * PT, 128) for s in range(2)]
        return jnp.concatenate(parts, axis=1)

    def term_copy(a, i):
        d, yd, xd, cd, own, at = owner_side(i)
        return own, lambda: remote(
            term_st.at[a, d], term_in.at[a, at], t_send.at[a, d], t_recv.at[a, at], yd * XC + xd * 2 + cd, z
        ), lambda: pltpu.make_async_copy(term_st.at[a, d], term_in.at[a, at], t_recv.at[a, at])

    def wait_slot(buf, sem, a, d):
        remote(buf.at[a, d], buf.at[a, d], sem.at[a, d], sem.at[a, d], blk, z).wait_recv()

    def put(a, col, g, value):
        value = value.astype(BF)
        for s in range(2):
            term_st[a, pl.ds(g * XC, XC), 2 * col + s] = value[:, s * 128:(s + 1) * 128].reshape(XC, PT, 128)

    def send_group(a, g):
        @pl.loop(0, XC)
        def _(q):
            own, far, near = term_copy(a, q * HALF + g)

            @pl.when(own)
            def _():
                near().start()

            @pl.when(jnp.logical_not(own))
            def _():
                far().start()

    @pl.loop(0, HALF)
    def _(g):
        @pl.loop(0, XC)
        def _(q):
            wait_slot(tile_in, d_recv, 0, g * XC + q)

        toks = pl.ds(pl.multiple_of(g * GT, GT), GT)
        for col in range(4):
            pre = dot(wide(0, col, g * XC, XC), wu[col], 1, 0)
            part = 0.5 * (1.0 + lax.erf(pre * INV_ROOT_TWO))
            keep = scale[col // 2, toks, (col % 2) * 128:(col % 2 + 1) * 128]
            hidden = (pre * part * keep).astype(BF)
            slope[col, toks] = (part + pre * jnp.exp(-0.5 * pre * pre) * INV_ROOT_TAU) * keep
            hid[col, toks] = hidden
            put(0, col, g, dot(hidden, wd[col], 1, 0))
        send_group(0, g)

    @pl.loop(0, HALF)
    def _(g):
        @pl.loop(0, XC)
        def _(q):
            wait_slot(tile_in, d_recv, 1, g * XC + q)

        toks = pl.ds(pl.multiple_of(g * GT, GT), GT)
        for col in range(4):
            grad = dot(wide(1, col, g * XC, XC), wd[col], 1, 1)
            grad = (grad * slope[col, toks]).astype(BF)
            gpre[col, toks] = grad
            put(1, col, g, dot(grad, wu[col], 1, 1))
        send_group(1, g)

    @pl.loop(0, 4)
    def _(col):
        grad_up = dot(wide(0, col, 0, ND), gpre[col], 0, 0).astype(BF)
        grad_dn = dot(hid[col], wide(1, col, 0, ND), 0, 0).astype(BF)
        rows = 128 // ZN
        for t in range(ZN):
            for s in range(2):
                gst[t, col, 0, s] = grad_up[s * 128 + t * rows:s * 128 + (t + 1) * rows, :]
                gst[t, col, 1, s] = grad_dn[t * rows:(t + 1) * rows, s * 128:(s + 1) * 128]

    def g_copy(o):
        t = lax.rem(z + o, ZN)
        return remote(gst.at[t], gin_z.at[z], g_send.at[o], g_recv.at[z], blk, t)

    for o in order:
        g_copy(o).start()
    gin_z[z] = gst[z]

    def o_copy(a, t):
        return remote(zo_st.at[a, t], zo_in.at[a, z], o_send.at[a, t], o_recv.at[a, z], blk, t)

    per = ZN // 2
    for a in range(2):
        @pl.loop(0, ND)
        def _(d):
            wait_slot(term_in, t_recv, a, d)

        @pl.loop(0, 2)
        def _(m):
            rows = per * RL * PT
            left = hot[pl.ds(pl.multiple_of(m * rows, rows), rows), :]
            total = dot(left, term_in[a].reshape(ND * 128, 128), 1, 0)
            zo_st[a, pl.ds(m * per, per)] = total.astype(BF).reshape(per, RL, PT, 128)
            for k in range(per):
                t = m * per + k

                @pl.when(t != z)
                def _():
                    o_copy(a, t).start()

        zo_in[a, z] = zo_st[a, z]

        if a == 0:
            for o in order:
                s = lax.rem(z + o, ZN)
                remote(gin_z.at[s], gin_z.at[s], g_send.at[o], g_recv.at[s], blk, z).wait_recv()
            for col in range(4):
                total = gin_z[0, col].astype(F32)
                for s in range(1, ZN):
                    total += gin_z[s, col].astype(F32)
                gsum[col] = total
            there = gsum.at[pl.ds(2 * (1 - up), 2)]
            q_copy = remote(there, gpart, p_send.at[3], p_recv.at[3], partner, z)
            q_copy.start()

    q_copy.wait_recv()
    for cl in range(2):
        own = gsum[2 * up + cl] + gpart[cl]
        for s in range(2):
            live = s < cnt_ref[cl]
            for ref, k in ((gup_ref, 0), (gdn_ref, 1)):
                ref[cl, s] = jnp.where(live, own[k, s], 0.0).astype(BF)

    for a, ref in enumerate((out_ref, gin_ref)):
        for o in order:
            s = lax.rem(z + o, ZN)
            remote(zo_in.at[a, s], zo_in.at[a, s], o_send.at[a, s], o_recv.at[a, s], blk, z).wait_recv()
        for s in range(ZN):
            for i in range(RL):
                ref[s * PT:(s + 1) * PT, i * 128:(i + 1) * 128] = zo_in[a, s, i]

    for o in range(1, XC):
        row_a(o).wait_send()
    for o in range(1, YN):
        row_b(o).wait_send()
    for copy in (*w_copies, m_copy, q_copy):
        copy.wait_send()
    for o in order:
        g_copy(o).wait_send()
        for a in range(2):
            z_copy(a, o).wait_send()
            o_copy(a, lax.rem(z + o, ZN)).wait_send()
    for a in range(2):
        @pl.loop(0, ND)
        def _(i):
            own, far, near = tile_copy(a, i)
            own_t, far_t, near_t = term_copy(a, i)

            @pl.when(jnp.logical_not(own))
            def _():
                far().wait_send()

            @pl.when(jnp.logical_not(own_t))
            def _():
                far_t().wait_send()


def per_device(inputs, grad_out, w_up, w_down, up_rows, slot_counts, keep_mask):
    tok, width = inputs.shape
    zn = lax.axis_size("tp")
    blocks = lax.axis_size("blk")
    xn = X_CHIPS
    yn = blocks // (2 * xn)
    pt, rl = tok // zn, width // 128
    half, xcn = yn // 2, 2 * xn
    nd, gt = half * xcn, xcn * pt
    rows = 128 // zn
    dims = (yn, xn, zn, pt, rl)
    vmem, smem = pl.BlockSpec(memory_space=pltpu.VMEM), pl.BlockSpec(memory_space=pltpu.SMEM)
    V, S = pltpu.VMEM, pltpu.SemaphoreType.DMA
    scratch = [
        V((2, zn, rl, pt, 128), BF),
        V((zn * rl, pt, 128), BF),
        V((zn * rl, pt, 128), BF),
        V((xcn, 8, 128), I32),
        V((yn, 8, 128), I32),
        pltpu.SMEM((yn, 8, 128), I32),
        V((4, 256, 128), BF),
        V((4, 128, 256), BF),
        V((yn, 16, gt), I32),
        V((2, half, 16, gt), I32),
        V((half, 16, gt), I32),
        V((2, half * gt, 256), F32),
        V((2, nd, 8, pt, 128), BF),
        V((2, nd, 8, pt, 128), BF),
        V((4, half * gt, 128), F32),
        V((4, half * gt, 128), BF),
        V((4, half * gt, 128), BF),
        V((2, nd, 8, pt, 128), BF),
        V((2, nd, 8, pt, 128), BF),
        V((nd, 8, 128), I32),
        V((zn * rl * pt, nd * 128), BF),
        V((2, zn, rl, pt, 128), BF),
        V((2, zn, rl, pt, 128), BF),
        V((zn, 4, 2, 2, rows, 128), BF),
        V((zn, 4, 2, 2, rows, 128), BF),
        V((4, 2, 2, rows, 128), F32),
        V((2, 2, 2, rows, 128), F32),
        S((2, zn)), S((2, zn)), S((xcn,)), S((xcn,)), S((yn,)), S((yn,)), S((4,)), S((4,)),
        S((2, nd)), S((2, nd)), S((2, nd)), S((2, nd)), S((2, zn)), S((2, zn)), S((zn,)), S((zn,)), S,
    ]
    shape = jax.ShapeDtypeStruct
    return pl.pallas_call(
        functools.partial(kernel, dims),
        out_shape=(
            shape(inputs.shape, BF), shape(inputs.shape, BF),
            shape((2, 2, rows, 128), BF), shape((2, 2, rows, 128), BF),
        ),
        in_specs=[vmem] * 5 + [smem] * 2,
        out_specs=(vmem,) * 4,
        scratch_shapes=scratch,
        compiler_params=pltpu.CompilerParams(
            collective_id=0, has_side_effects=True, vmem_limit_bytes=48 * 1024 * 1024
        ),
        cost_estimate=pl.CostEstimate(flops=10**10, bytes_accessed=10**7, transcendentals=10**6),
    )(inputs, grad_out, w_up, w_down, keep_mask.T, up_rows, slot_counts)


def solution(mesh):
    return jax.shard_map(
        per_device,
        mesh=mesh,
        in_specs=(
            P("blk", "tp"),
            P("blk", "tp"),
            P("blk", None, None, None),
            P("blk", None, None, None),
            P("blk", None),
            P("blk"),
            P(None, "blk"),
        ),
        out_specs=(
            P("blk", "tp"),
            P("blk", "tp"),
            P("blk", None, "tp", None),
            P("blk", None, "tp", None),
        ),
        check_vma=False,
    )
```

time: 341 us -> 106 us (0.31)
  the two profiles are of different devices: /device:TPU:6 before, /device:TPU:1 now
where the time goes in v1:
time: 106 us
  Pallas kernels  96.8 us (91%)
  local copies, waits for them, and re-layouts  8.04 us (8%)
    pallas_call x1, Pallas kernels, per_device(): pl.pallas_call(functools.partial(kernel, dims), out_shape=(shape(inputs.s...  96.8 us
    unnamed x18, local copies, waits for them, and re-layouts  8.04 us

profile of v1, /device:TPU:1, one launch (start us, length us, event | category | flops | bytes accessed | tf_op | source)
XLA Modules:
  0.0 105.6 jit_solution(5091749893681398749)
XLA Ops:
  0.6 0.0 copy-start.6
  0.6 0.0 copy-start.5
  0.7 0.6 copy-done.6
  1.3 0.0 copy-done.5
  1.3 0.0 copy-start
  1.3 1.0 copy-done
  2.4 0.0 copy-start.1
  2.4 0.9 copy-done.1
  3.3 0.0 copy-start.2
  3.3 0.9 copy-done.2
  4.3 0.0 copy-start.3
  4.3 0.9 copy-done.3
  5.2 0.0 copy-start.4
  5.2 0.9 copy-done.4
  6.1 96.8 %shard_map.102 = (bf16[128,1024]{1,0:T(8,128)(2,1)S(1)}, bf16[128,1024]{1,0:T(8,128)(2,1)S(1)}, bf16[2,2,16,128]{3,2,1,0:T(8,128)(2,1)S(1)}, bf16[2,2,16,128]{3,2,1,0:T(8,128)(2,1)S(1)}) custom-call(bf16[128,1024]{1,0:T(8,128)(2,1)S(1)} %copy-done.1, bf16[128,1024]{1,0:T(8,128)(2,1)S(1)} %copy-done.2, bf16[2,2,128,128]{3,2,1,0:T(8,128)(2,1)S(1)} %copy-done.3, ...), custom_call_target="tpu_custom_call" | custom-call | flops 10000000000 | bytes 10000000 | tf_op jit(solution)/shard_map/pallas_call | solution.py:441
  102.9 0.7 copy.15
  103.6 0.7 copy.16
  104.3 0.6 copy.17
  105.0 0.6 copy.18
Async XLA Ops:
  0.6 0.7 copy-start.6
  0.6 0.7 copy-start.5
  1.3 1.0 copy-start
  2.4 0.9 copy-start.1
  3.3 0.9 copy-start.2
  4.3 0.9 copy-start.3
  5.2 0.9 copy-start.4

commit v2 on v1

v2 whole, which is shorter than its diff:
```python
import functools

import jax
import jax.numpy as jnp
from jax import lax
from jax.experimental import pallas as pl
from jax.experimental.pallas import tpu as pltpu
from jax.sharding import PartitionSpec as P

INV_ROOT_TWO = 0.7071067811865476
INV_ROOT_TAU = 0.3989422804014327
KEEP_SCALE = 1.25
MESH = pl.DeviceIdType.MESH
X_CHIPS = 4
BF = jnp.bfloat16
F32 = jnp.float32
I32 = jnp.int32


def dot(a, b, ca, cb):
    return lax.dot_general(a, b, (((ca,), (cb,)), ((), ())), preferred_element_type=F32)


def iota(shape, dim):
    return lax.broadcasted_iota(I32, shape, dim)


def hop(value, step, count):
    there = value + step
    there = jnp.where(there >= count, there - count, there)
    return jnp.where(there < 0, there + count, there)


def split(value, count):
    shift = count.bit_length() - 1
    assert count == 1 << shift
    return jnp.right_shift(value, shift), jnp.bitwise_and(value, count - 1)


def kernel(
    dims,
    x_hbm, dy_hbm, wu_hbm, wd_hbm, keep_hbm, rows_ref, cnt_ref,
    out_ref, gin_ref, gup_ref, gdn_ref,
    x_ref, dy_ref, wu_ref, wd_ref, keep_ref, zst, full_x, full_dy, rows_a, rows_b, rows_s, wu, wd, tokw, maskw, mask_st, scale,
    tile_st, tile_in, slope, hid, gpre, term_st, term_in, lanes, hot,
    zo_st, zo_in, gst, gin_z, gsum, gpart,
    z_send, z_recv, a_send, a_recv, b_send, b_recv, p_send, p_recv,
    d_send, d_recv, t_send, t_recv, o_send, o_recv, g_send, g_recv, l_sem, in_sem, v_send, v_recv,
):
    YN, XN, ZN, PT, RL = dims
    XC = XN * 2
    HALF = YN // 2
    LO = HALF // 2 - 1
    ND = HALF * XC
    RB = RL * ZN
    GT = XC * PT
    blk, z = lax.axis_index("blk"), lax.axis_index("tp")
    c = lax.rem(blk, 2)
    x = lax.rem(blk // 2, XN)
    y = blk // XC
    xc = x * 2 + c
    up = jnp.where(y >= HALF, 1, 0)
    partner = hop(y, HALF, YN) * XC + xc

    def remote(src, dst, ss, rs, b, t):
        return pltpu.make_async_remote_copy(
            src_ref=src, dst_ref=dst, send_sem=ss, recv_sem=rs, device_id=(b, t), device_id_type=MESH
        )

    fetch = [
        pltpu.make_async_copy(src, dst, in_sem.at[k])
        for k, (src, dst) in enumerate(
            ((x_hbm, x_ref), (dy_hbm, dy_ref), (wu_hbm, wu_ref), (wd_hbm, wd_ref), (keep_hbm, keep_ref))
        )
    ]
    for one in fetch:
        one.start()

    barrier = pltpu.get_barrier_semaphore()
    peers = []
    for dy in range(-(HALF // 2), YN - HALF // 2):
        for xo in range(XN):
            for co in range(2):
                if (dy, xo, co) == (0, 0, 0):
                    continue
                if abs(dy) <= HALF // 2 or (xo, co) == (0, 0):
                    peers.append((hop(y, dy, YN) * XC + hop(x, xo, XN) * 2 + hop(c, co, 2), z))
    for zo in range(1, ZN):
        peers.append((blk, hop(z, zo, ZN)))
    for b, t in peers:
        pl.semaphore_signal(barrier, inc=1, device_id=(b, t), device_id_type=MESH)

    full = (full_x, full_dy)
    lane = iota((8, 128), 1)
    mine = jnp.where(lane == 0, rows_ref[0, 0], jnp.where(lane == 1, rows_ref[0, 1],
                     jnp.where(lane == 2, rows_ref[1, 0], rows_ref[1, 1])))
    rows_a[xc] = mine
    for a, ref in enumerate((x_ref, dy_ref)):
        fetch[a].wait()
        for t in range(ZN):
            for i in range(RL):
                zst[a, t, i] = ref[t * PT:(t + 1) * PT, i * 128:(i + 1) * 128]
        full[a][pl.ds(z * RL, RL)] = zst[a, z]
    fetch[2].wait()
    fetch[3].wait()
    for cl in range(2):
        for s in range(2):
            live = s < cnt_ref[cl]
            wu[2 * up + cl, s * 128:(s + 1) * 128, :] = jnp.where(live, wu_ref[cl, s], jnp.zeros((), BF))
            wd[2 * up + cl, :, s * 128:(s + 1) * 128] = jnp.where(live, wd_ref[cl, s], jnp.zeros((), BF))
    pl.semaphore_wait(barrier, len(peers))

    def row_a(o):
        q = hop(xc, o, XC)
        return remote(rows_a.at[xc], rows_a.at[xc], a_send.at[o], a_recv.at[xc], y * XC + q, z)

    for o in range(1, XC):
        row_a(o).start()

    order = [o for k in range(1, ZN // 2 + 1) for o in dict.fromkeys((k, ZN - k))]

    def z_copy(a, o):
        t = hop(z, o, ZN)
        return remote(zst.at[a, t], full[a].at[pl.ds(z * RL, RL)], z_send.at[a], z_recv.at[a], blk, t)

    for o in order:
        z_copy(0, o).start()

    def w_slice(k, half, at):
        rows = (256, 128)[k] // ZN
        return (wu, wd)[k].at[pl.ds(2 * half, 2), pl.ds(pl.multiple_of(at * rows, rows), rows)]

    w_copies = [
        remote(w_slice(k, up, z), w_slice(k, up, z), p_send.at[k], p_recv.at[k], partner, z) for k in range(2)
    ]
    for w_copy in w_copies:
        w_copy.start()

    def wait_a(o):
        q = hop(xc, o, XC)
        remote(rows_a.at[q], rows_a.at[q], a_send.at[o], a_recv.at[q], blk, z).wait_recv()

    for o in range(1, XC):
        wait_a(o)
    sub = iota((8, 128), 0)
    packed = rows_a[0]
    for q in range(1, XC):
        packed = jnp.where(sub == q, rows_a[q], packed)
    rows_b[y] = packed

    def row_b(o):
        q = hop(y, o, YN)
        return remote(rows_b.at[y], rows_b.at[y], b_send.at[o], b_recv.at[y], q * XC + xc, z)

    for o in range(1, YN):
        row_b(o).start()
    for o in range(1, YN):
        q = hop(y, o, YN)
        remote(rows_b.at[q], rows_b.at[q], b_send.at[o], b_recv.at[q], blk, z).wait_recv()
    to_scalar = pltpu.make_async_copy(rows_b, rows_s, l_sem)
    to_scalar.start()
    to_scalar.wait()

    def token_side(j, xo, co):
        xd, cd = hop(x, xo, XN), hop(c, co, 2)
        yd = hop(y, LO - j + cd, YN)
        return j * XC + xd * 2 + cd, yd, xd * 2 + cd, j * XC + xc

    def owner_side(j, xo, co):
        xd, cd = hop(x, xo, XN), hop(c, co, 2)
        yd = hop(y, j - LO - c, YN)
        return j * XC + xd * 2 + cd, yd, xd * 2 + cd, j * XC + xc

    def send_to(side, st, into, sends, recvs, a, j, xo, co):
        d, yd, xcd, at = side(j, xo, co)
        own = (j == LO + c) & (xo == 0)

        def near():
            pltpu.make_async_copy(st.at[a, d], into.at[a, at], recvs.at[a, j]).start()

        def far():
            remote(st.at[a, d], into.at[a, at], sends.at[a], recvs.at[a, j], yd * XC + xcd, z).start()

        if co == 0:
            pl.when(own)(near)
            pl.when(jnp.logical_not(own))(far)
        else:
            far()

    def slot_rows(yd, xcd):
        low = jnp.where(yd >= HALF, yd - HALF, yd)
        return [rows_s[low + HALF * (k // 4), xcd, k % 4] for k in range(8)]

    def wait_z(a):
        others = full[a].at[pl.ds(0, (ZN - 1) * RL)]
        remote(others, others, z_send.at[a], z_recv.at[a], blk, z).wait_recv()

    def dispatch(a):
        @pl.loop(0, XN)
        def _(xo):
            for co in range(2):
                for j in range(HALF):
                    d, yd, xcd, at = token_side(j, xo, co)
                    for k, row in enumerate(slot_rows(yd, xcd)):
                        tile_st[a, d, k] = full[a][row]
                    send_to(token_side, tile_st, tile_in, d_send, d_recv, a, j, xo, co)

    wait_z(0)
    for o in order:
        z_copy(1, o).start()
    for k in range(2):
        mine = w_slice(k, 1 - up, z)
        remote(mine, mine, p_send.at[k], p_recv.at[k], partner, z).wait_recv()
        for o in order:
            remote(mine, mine, v_send.at[k], v_recv.at[k], blk, hop(z, o, ZN)).start()
    dispatch(0)

    span = XC * ZN * PT
    r, l = iota((span, GT), 0), iota((span, GT), 1)
    share = ZN * PT
    (r, rest), (l, near) = split(r, share), split(l, PT)
    pick = jnp.where((r == l) & (rest == z * PT + near), 1.0, 0.0).astype(BF)
    fetch[4].wait()
    for g in range(YN):
        words = keep_ref[:, g * span:(g + 1) * span]
        low = jnp.bitwise_and(words, 255).astype(F32).astype(BF)
        high = jnp.right_shift(words, 8).astype(F32).astype(BF)
        found = dot(jnp.concatenate([low, high], axis=0), pick, 1, 0).astype(I32)
        tokw[g] = found[:16] + found[16:] * 256
    for j in range(HALF):
        maskw[up, j] = tokw[hop(y, j - LO - c, YN)]
        mask_st[j] = tokw[hop(hop(y, HALF, YN), j - LO - c, YN)]
    m_copy = remote(mask_st, maskw.at[up], p_send.at[2], p_recv.at[2], partner, z)
    m_copy.start()

    wait_z(1)
    dispatch(1)

    piece, near_token = split(lane, PT)

    @pl.loop(0, XN)
    def _(xo):
        for co in range(2):
            for j in range(HALF):
                d, yd, xcd, at = token_side(j, xo, co)
                value = near_token
                for k, row in enumerate(slot_rows(yd, xcd)):
                    value = jnp.where(piece == k, row * PT + near_token, value)
                lanes[d] = value

    @pl.loop(0, ND)
    def _(d):
        want = lanes[d][0:1, :]
        at = pl.ds(pl.multiple_of(d * 128, 128), 128)
        hot[:, at] = jnp.where(iota((RB * PT, 128), 0) == want, 1.0, 0.0).astype(BF)

    m_wait = remote(mask_st, maskw.at[1 - up], p_send.at[2], p_recv.at[2], partner, z)
    m_wait.wait_recv()
    er, el = iota((32, 256), 0), iota((32, 256), 1)
    (word, bit), (_, which) = split(el, 16), split(er, 16)
    spread = jnp.where((word == which) & ((bit >= 8) == (er >= 16)), 1.0, 0.0).astype(BF)
    shift = split(iota((GT, 256), 1), 8)[1]
    for h in range(2):
        for j in range(HALF):
            words = maskw[h, j]
            low = jnp.bitwise_and(words, 255).astype(F32).astype(BF)
            high = jnp.right_shift(words, 8).astype(F32).astype(BF)
            found = dot(jnp.concatenate([low, high], axis=0), spread, 0, 0).astype(I32)
            keep = jnp.bitwise_and(jnp.right_shift(found, shift), 1)
            scale[h, j * GT:(j + 1) * GT, :] = keep.astype(F32) * KEEP_SCALE
    def seven(k):
        rows = (256, 128)[k] // ZN
        return (wu, wd)[k].at[pl.ds(0, 2), pl.ds(0, (ZN - 1) * rows)]

    for k in range(2):
        remote(seven(k), seven(k), v_send.at[k], v_recv.at[k], blk, z).wait_recv()

    def wide(a, col, start, count):
        parts = [tile_in[a, pl.ds(start, count), 2 * col + s].reshape(count * PT, 128) for s in range(2)]
        return jnp.concatenate(parts, axis=1)

    def wait_group(buf, sem, a, g):
        block = buf.at[a, pl.ds(g * XC, XC)]
        remote(block, block, sem.at[a, g], sem.at[a, g], blk, z).wait_recv()

    def put(a, col, g, value):
        value = value.astype(BF)
        for s in range(2):
            term_st[a, pl.ds(g * XC, XC), 2 * col + s] = value[:, s * 128:(s + 1) * 128].reshape(XC, PT, 128)

    def send_group(a, g):
        @pl.loop(0, XN)
        def _(xo):
            for co in range(2):
                send_to(owner_side, term_st, term_in, t_send, t_recv, a, g, xo, co)

    @pl.loop(0, HALF)
    def _(g):
        wait_group(tile_in, d_recv, 0, g)
        toks = pl.ds(pl.multiple_of(g * GT, GT), GT)
        for col in range(4):
            pre = dot(wide(0, col, g * XC, XC), wu[col], 1, 0)
            part = 0.5 * (1.0 + lax.erf(pre * INV_ROOT_TWO))
            keep = scale[col // 2, toks, (col % 2) * 128:(col % 2 + 1) * 128]
            hidden = (pre * part * keep).astype(BF)
            slope[col, toks] = (part + pre * jnp.exp(-0.5 * pre * pre) * INV_ROOT_TAU) * keep
            hid[col, toks] = hidden
            put(0, col, g, dot(hidden, wd[col], 1, 0))
        send_group(0, g)

    @pl.loop(0, HALF)
    def _(g):
        wait_group(tile_in, d_recv, 1, g)
        toks = pl.ds(pl.multiple_of(g * GT, GT), GT)
        for col in range(4):
            grad = dot(wide(1, col, g * XC, XC), wd[col], 1, 1)
            grad = (grad * slope[col, toks]).astype(BF)
            gpre[col, toks] = grad
            put(1, col, g, dot(grad, wu[col], 1, 1))
        send_group(1, g)

    @pl.loop(0, 4)
    def _(col):
        grad_up = dot(wide(0, col, 0, ND), gpre[col], 0, 0).astype(BF)
        grad_dn = dot(hid[col], wide(1, col, 0, ND), 0, 0).astype(BF)
        rows = 128 // ZN
        for t in range(ZN):
            for s in range(2):
                gst[t, col, 0, s] = grad_up[s * 128 + t * rows:s * 128 + (t + 1) * rows, :]
                gst[t, col, 1, s] = grad_dn[t * rows:(t + 1) * rows, s * 128:(s + 1) * 128]

    def g_copy(o):
        t = hop(z, o, ZN)
        return remote(gst.at[t], gin_z.at[z], g_send, g_recv, blk, t)

    for o in order:
        g_copy(o).start()
    gin_z[z] = gst[z]

    def o_copy(a, t):
        return remote(zo_st.at[a, t], zo_in.at[a, z], o_send.at[a], o_recv.at[a], blk, t)

    per = ZN // 2
    for a in range(2):
        for j in range(HALF):
            wait_group(term_in, t_recv, a, j)

        @pl.loop(0, 2)
        def _(m):
            rows = per * RL * PT
            left = hot[pl.ds(pl.multiple_of(m * rows, rows), rows), :]
            total = dot(left, term_in[a].reshape(ND * 128, 128), 1, 0)
            zo_st[a, pl.ds(m * per, per)] = total.astype(BF).reshape(per, RL, PT, 128)
            for k in range(per):
                t = m * per + k

                @pl.when(t != z)
                def _():
                    o_copy(a, t).start()

        zo_in[a, z] = zo_st[a, z]

    most = pl.ds(0, ZN - 1)
    remote(gin_z.at[most], gin_z.at[most], g_send, g_recv, blk, z).wait_recv()
    for col in range(4):
        total = gin_z[0, col].astype(F32)
        for s in range(1, ZN):
            total += gin_z[s, col].astype(F32)
        gsum[col] = total
    there = gsum.at[pl.ds(2 * (1 - up), 2)]
    q_copy = remote(there, gpart, p_send.at[3], p_recv.at[3], partner, z)
    q_copy.start()

    for a, ref in enumerate((out_ref, gin_ref)):
        remote(zo_in.at[a, most], zo_in.at[a, most], o_send.at[a], o_recv.at[a], blk, z).wait_recv()
        for s in range(ZN):
            for i in range(RL):
                ref[s * PT:(s + 1) * PT, i * 128:(i + 1) * 128] = zo_in[a, s, i]

    q_copy.wait_recv()
    for cl in range(2):
        own = gsum[2 * up + cl] + gpart[cl]
        for s in range(2):
            live = s < cnt_ref[cl]
            for ref, k in ((gup_ref, 0), (gdn_ref, 1)):
                ref[cl, s] = jnp.where(live, own[k, s], 0.0).astype(BF)

    for o in range(1, XC):
        row_a(o).wait_send()
    for o in range(1, YN):
        row_b(o).wait_send()
    for copy in (*w_copies, m_copy, q_copy):
        copy.wait_send()
    sent = pl.ds(0, ND - 1)
    for a in range(2):
        for buf, sem in (
            (zst.at[a, most], z_send), (zo_st.at[a, most], o_send),
            (tile_st.at[a, sent], d_send), (term_st.at[a, sent], t_send),
        ):
            remote(buf, buf, sem.at[a], sem.at[a], blk, z).wait_send()
    remote(gst.at[most], gst.at[most], g_send, g_recv, blk, z).wait_send()
    for k in range(2):
        remote(seven(k), seven(k), v_send.at[k], v_recv.at[k], blk, z).wait_send()


def place(*refs):
    for src, dst in zip(refs[:4], refs[4:]):
        dst[...] = src[...]


def per_device(inputs, grad_out, w_up, w_down, up_rows, slot_counts, keep_mask):
    tok, width = inputs.shape
    zn = lax.axis_size("tp")
    blocks = lax.axis_size("blk")
    xn = X_CHIPS
    yn = blocks // (2 * xn)
    pt, rl = tok // zn, width // 128
    half, xcn = yn // 2, 2 * xn
    nd, gt = half * xcn, xcn * pt
    rows = 128 // zn
    dims = (yn, xn, zn, pt, rl)
    vmem, smem = pl.BlockSpec(memory_space=pltpu.VMEM), pl.BlockSpec(memory_space=pltpu.SMEM)
    V, S = pltpu.VMEM, pltpu.SemaphoreType.DMA
    scratch = [
        V(inputs.shape, BF), V(inputs.shape, BF), V(w_up.shape, BF), V(w_down.shape, BF),
        V(keep_mask.shape[::-1], I32),
        V((2, zn, rl, pt, 128), BF),
        V((zn * rl, pt, 128), BF),
        V((zn * rl, pt, 128), BF),
        V((xcn, 8, 128), I32),
        V((yn, 8, 128), I32),
        pltpu.SMEM((yn, 8, 128), I32),
        V((4, 256, 128), BF),
        V((4, 128, 256), BF),
        V((yn, 16, gt), I32),
        V((2, half, 16, gt), I32),
        V((half, 16, gt), I32),
        V((2, half * gt, 256), F32),
        V((2, nd, 8, pt, 128), BF),
        V((2, nd, 8, pt, 128), BF),
        V((4, half * gt, 128), F32),
        V((4, half * gt, 128), BF),
        V((4, half * gt, 128), BF),
        V((2, nd, 8, pt, 128), BF),
        V((2, nd, 8, pt, 128), BF),
        V((nd, 8, 128), I32),
        V((zn * rl * pt, nd * 128), BF),
        V((2, zn, rl, pt, 128), BF),
        V((2, zn, rl, pt, 128), BF),
        V((zn, 4, 2, 2, rows, 128), BF),
        V((zn, 4, 2, 2, rows, 128), BF),
        V((4, 2, 2, rows, 128), F32),
        V((2, 2, 2, rows, 128), F32),
        S((2,)), S((2,)), S((xcn,)), S((xcn,)), S((yn,)), S((yn,)), S((4,)), S((4,)),
        S((2,)), S((2, half)), S((2,)), S((2, half)), S((2,)), S((2,)), S, S, S, S((5,)), S((2,)), S((2,)),
    ]
    shape = jax.ShapeDtypeStruct
    shapes = (
        shape(inputs.shape, BF), shape(inputs.shape, BF),
        shape((2, 2, rows, 128), BF), shape((2, 2, rows, 128), BF),
    )
    results = pl.pallas_call(
        functools.partial(kernel, dims),
        out_shape=shapes,
        in_specs=[pl.BlockSpec(memory_space=pl.ANY)] * 5 + [smem] * 2,
        out_specs=(vmem,) * 4,
        scratch_shapes=scratch,
        compiler_params=pltpu.CompilerParams(
            collective_id=0, has_side_effects=True, vmem_limit_bytes=56 * 1024 * 1024
        ),
        cost_estimate=pl.CostEstimate(flops=10**10, bytes_accessed=10**7, transcendentals=10**6),
    )(inputs, grad_out, w_up, w_down, keep_mask.T, up_rows, slot_counts)
    return pl.pallas_call(place, out_shape=shapes, in_specs=[vmem] * 4, out_specs=(vmem,) * 4)(*results)


def solution(mesh):
    return jax.shard_map(
        per_device,
        mesh=mesh,
        in_specs=(
            P("blk", "tp"),
            P("blk", "tp"),
            P("blk", None, None, None),
            P("blk", None, None, None),
            P("blk", None),
            P("blk"),
            P(None, "blk"),
        ),
        out_specs=(
            P("blk", "tp"),
            P("blk", "tp"),
            P("blk", None, "tp", None),
            P("blk", None, "tp", None),
        ),
        check_vma=False,
    )
```

time: 106 us -> 88.1 us (0.83)
  the two profiles are of different devices: /device:TPU:1 before, /device:TPU:6 now
where the time goes in v2:
time: 88.1 us; the launch traced here: 87.5 us
  Pallas kernels  86.8 us (99%)
    pallas_call x1, Pallas kernels, per_device(): pl.pallas_call(functools.partial(kernel, dims), out_shape=shapes, in_spec...  85 us
    pallas_call x1, Pallas kernels, per_device(): pl.pallas_call(place, out_shape=shapes, in_specs=[vmem] * 4, out_specs=(v...  1.85 us

profile of v2, /device:TPU:6, one launch (start us, length us, event | category | flops | bytes accessed | tf_op | source)
XLA Modules:
  0.0 87.5 jit_solution(6644814773437037165)
XLA Ops:
  0.6 85.0 %shard_map.102 = (bf16[128,1024]{1,0:T(8,128)(2,1)}, bf16[128,1024]{1,0:T(8,128)(2,1)}, bf16[2,2,16,128]{3,2,1,0:T(8,128)(2,1)}, bf16[2,2,16,128]{3,2,1,0:T(8,128)(2,1)}) custom-call(bf16[128,1024]{1,0:T(8,128)(2,1)} %x_hbm.1, bf16[128,1024]{1,0:T(8,128)(2,1)} %dy_hbm.1, bf16[2,2,128,128]{3,2,1,0:T(8,128)(2,1)} %wu_hbm.1, bf16[2,2,128,128]{3,2,1,0:T(8,128)(2,1)} %wd_hbm.1, ...), custom_call_target="tpu_custom_call" | custom-call | flops 10000000000 | bytes 10000000 | tf_op jit(solution)/shard_map/pallas_call | solution.py:462
  85.6 1.8 %shard_map.103 = (bf16[128,1024]{1,0:T(8,128)(2,1)}, bf16[128,1024]{1,0:T(8,128)(2,1)}, bf16[2,2,16,128]{3,2,1,0:T(8,128)(2,1)}, bf16[2,2,16,128]{3,2,1,0:T(8,128)(2,1)}) custom-call(bf16[128,1024]{1,0:T(8,128)(2,1)} %get-tuple-element.8.refs_0_, bf16[128,1024]{1,0:T(8,128)(2,1)} %get-tuple-element.9.refs_1_, ...), custom_call_target="tpu_custom_call" | custom-call | tf_op jit(solution)/shard_map/pallas_call | solution.py:473

commit v3 on v2

--- a/solution.py
+++ b/solution.py
@@ -43,7 +43,7 @@
     out_ref, gin_ref, gup_ref, gdn_ref,
     x_ref, dy_ref, wu_ref, wd_ref, keep_ref, zst, full_x, full_dy, rows_a, rows_b, rows_s, wu, wd, tokw, maskw, mask_st, scale,
     tile_st, tile_in, slope, hid, gpre, term_st, term_in, lanes, hot,
-    zo_st, zo_in, gst, gin_z, gsum, gpart,
+    acc, zo_st, zo_in, gst, gin_z, gsum, gpart,
     z_send, z_recv, a_send, a_recv, b_send, b_recv, p_send, p_recv,
     d_send, d_recv, t_send, t_recv, o_send, o_recv, g_send, g_recv, l_sem, in_sem, v_send, v_recv,
 ):
@@ -161,6 +161,8 @@
     to_scalar.start()
     to_scalar.wait()
 
+    x_order = [xo for xo in (2, 1, 0, 3) if xo < XN]
+
     def token_side(j, xo, co):
         xd, cd = hop(x, xo, XN), hop(c, co, 2)
         yd = hop(y, LO - j + cd, YN)
@@ -173,7 +175,7 @@
 
     def send_to(side, st, into, sends, recvs, a, j, xo, co):
         d, yd, xcd, at = side(j, xo, co)
-        own = (j == LO + c) & (xo == 0)
+        own = j == LO + c
 
         def near():
             pltpu.make_async_copy(st.at[a, d], into.at[a, at], recvs.at[a, j]).start()
@@ -181,7 +183,7 @@
         def far():
             remote(st.at[a, d], into.at[a, at], sends.at[a], recvs.at[a, j], yd * XC + xcd, z).start()
 
-        if co == 0:
+        if co == 0 and xo == 0:
             pl.when(own)(near)
             pl.when(jnp.logical_not(own))(far)
         else:
@@ -196,10 +198,10 @@
         remote(others, others, z_send.at[a], z_recv.at[a], blk, z).wait_recv()
 
     def dispatch(a):
-        @pl.loop(0, XN)
-        def _(xo):
+        @pl.loop(0, HALF)
+        def _(j):
             for co in range(2):
-                for j in range(HALF):
+                for xo in x_order:
                     d, yd, xcd, at = token_side(j, xo, co)
                     for k, row in enumerate(slot_rows(yd, xcd)):
                         tile_st[a, d, k] = full[a][row]
@@ -289,9 +291,8 @@
             term_st[a, pl.ds(g * XC, XC), 2 * col + s] = value[:, s * 128:(s + 1) * 128].reshape(XC, PT, 128)
 
     def send_group(a, g):
-        @pl.loop(0, XN)
-        def _(xo):
-            for co in range(2):
+        for co in range(2):
+            for xo in x_order:
                 send_to(owner_side, term_st, term_in, t_send, t_recv, a, g, xo, co)
 
     @pl.loop(0, HALF)
@@ -340,24 +341,35 @@
     def o_copy(a, t):
         return remote(zo_st.at[a, t], zo_in.at[a, z], o_send.at[a], o_recv.at[a], blk, t)
 
-    per = ZN // 2
+    rows = RL * PT
+    deep = XC * 128
+
+    def chosen(a, g, t, count):
+        left = hot[pl.ds(pl.multiple_of(t * rows, rows), count * rows), pl.ds(pl.multiple_of(g * deep, deep), deep)]
+        return dot(left, term_in[a, pl.ds(g * XC, XC)].reshape(deep, 128), 1, 0)
+
     for a in range(2):
-        for j in range(HALF):
-            wait_group(term_in, t_recv, a, j)
-
-        @pl.loop(0, 2)
+        wait_group(term_in, t_recv, a, 0)
+
+        @pl.loop(0, ZN // 2)
         def _(m):
-            rows = per * RL * PT
-            left = hot[pl.ds(pl.multiple_of(m * rows, rows), rows), :]
-            total = dot(left, term_in[a].reshape(ND * 128, 128), 1, 0)
-            zo_st[a, pl.ds(m * per, per)] = total.astype(BF).reshape(per, RL, PT, 128)
-            for k in range(per):
-                t = m * per + k
-
-                @pl.when(t != z)
-                def _():
-                    o_copy(a, t).start()
-
+            acc[pl.ds(pl.multiple_of(m * 2 * rows, rows), 2 * rows)] = chosen(a, 0, 2 * m, 2)
+
+        @pl.loop(1, HALF - 1)
+        def _(g):
+            wait_group(term_in, t_recv, a, g)
+
+            @pl.loop(0, ZN // 2)
+            def _(m):
+                acc[pl.ds(pl.multiple_of(m * 2 * rows, rows), 2 * rows)] += chosen(a, g, 2 * m, 2)
+
+        wait_group(term_in, t_recv, a, HALF - 1)
+        for o in (*order[::-1], 0):
+            t = hop(z, o, ZN)
+            total = acc[pl.ds(pl.multiple_of(t * rows, rows), rows)] + chosen(a, HALF - 1, t, 1)
+            zo_st[a, t] = total.astype(BF).reshape(RL, PT, 128)
+            if o:
+                o_copy(a, t).start()
         zo_in[a, z] = zo_st[a, z]
 
     most = pl.ds(0, ZN - 1)
@@ -445,6 +457,7 @@
         V((2, nd, 8, pt, 128), BF),
         V((nd, 8, 128), I32),
         V((zn * rl * pt, nd * 128), BF),
+        V((zn * rl * pt, 128), F32),
         V((2, zn, rl, pt, 128), BF),
         V((2, zn, rl, pt, 128), BF),
         V((zn, 4, 2, 2, rows, 128), BF),
@@ -461,7 +474,7 @@
     )
     results = pl.pallas_call(
         functools.partial(kernel, dims),
-        out_shape=shapes,
+        out_shape=tuple(pltpu.VMEM(one.shape, one.dtype) for one in shapes),
         in_specs=[pl.BlockSpec(memory_space=pl.ANY)] * 5 + [smem] * 2,
         out_specs=(vmem,) * 4,
         scratch_shapes=scratch,
@@ -470,6 +483,7 @@
         ),
         cost_estimate=pl.CostEstimate(flops=10**10, bytes_accessed=10**7, transcendentals=10**6),
     )(inputs, grad_out, w_up, w_down, keep_mask.T, up_rows, slot_counts)
+    results = [pltpu.with_memory_space_constraint(one, pltpu.VMEM) for one in results]
     return pl.pallas_call(place, out_shape=shapes, in_specs=[vmem] * 4, out_specs=(vmem,) * 4)(*results)
 
 

time: 88.1 us -> 85.5 us (0.970)
  Pallas kernels: 86.8 us -> 84.4 us
    pallas_call x1, Pallas kernels: 85 us -> 83.6 us  [per_device(): pl.pallas_call(functools.partial(kernel, dims), out_shape=tuple((pltpu.VM...]
    pallas_call x1, Pallas kernels: 1.85 us -> 0.83 us  [per_device(): pl.pallas_call(place, out_shape=shapes, in_specs=[vmem] * 4, out_specs=(v...]
where the time goes in v3:
time: 85.5 us; the launch traced here: 85 us
  Pallas kernels  84.4 us (99%)
    pallas_call x1, Pallas kernels, per_device(): pl.pallas_call(functools.partial(kernel, dims), out_shape=tuple((pltpu.VM...  83.6 us

profile of v3, /device:TPU:6, one launch (start us, length us, event | category | flops | bytes accessed | tf_op | source)
XLA Modules:
  0.0 85.0 jit_solution(16475614979437341322)
XLA Ops:
  0.6 83.6 %shard_map.102 = (bf16[128,1024]{1,0:T(8,128)(2,1)S(1)}, bf16[128,1024]{1,0:T(8,128)(2,1)S(1)}, bf16[2,2,16,128]{3,2,1,0:T(8,128)(2,1)S(1)}, bf16[2,2,16,128]{3,2,1,0:T(8,128)(2,1)S(1)}) custom-call(bf16[128,1024]{1,0:T(8,128)(2,1)} %x_hbm.1, bf16[128,1024]{1,0:T(8,128)(2,1)} %dy_hbm.1, bf16[2,2,128,128]{3,2,1,0:T(8,128)(2,1)} %wu_hbm.1, ...), custom_call_target="tpu_custom_call" | custom-call | flops 10000000000 | bytes 10000000 | tf_op jit(solution)/shard_map/pallas_call | solution.py:475
  84.2 0.8 shard_map.103

commit v4 on v3

--- a/solution.py
+++ b/solution.py
@@ -76,17 +76,15 @@
     for one in fetch:
         one.start()
 
+    order = [o for k in range(1, ZN // 2 + 1) for o in dict.fromkeys((k, ZN - k))]
     barrier = pltpu.get_barrier_semaphore()
     peers = []
-    for dy in range(-(HALF // 2), YN - HALF // 2):
-        for xo in range(XN):
-            for co in range(2):
-                if (dy, xo, co) == (0, 0, 0):
-                    continue
-                if abs(dy) <= HALF // 2 or (xo, co) == (0, 0):
-                    peers.append((hop(y, dy, YN) * XC + hop(x, xo, XN) * 2 + hop(c, co, 2), z))
-    for zo in range(1, ZN):
+    for zo in order:
         peers.append((blk, hop(z, zo, ZN)))
+    for o in range(1, XC):
+        peers.append((y * XC + hop(xc, o, XC), z))
+    for o in range(1, YN):
+        peers.append((hop(y, o, YN) * XC + xc, z))
     for b, t in peers:
         pl.semaphore_signal(barrier, inc=1, device_id=(b, t), device_id_type=MESH)
 
@@ -117,7 +115,6 @@
     for o in range(1, XC):
         row_a(o).start()
 
-    order = [o for k in range(1, ZN // 2 + 1) for o in dict.fromkeys((k, ZN - k))]
 
     def z_copy(a, o):
         t = hop(z, o, ZN)
@@ -364,7 +361,7 @@
                 acc[pl.ds(pl.multiple_of(m * 2 * rows, rows), 2 * rows)] += chosen(a, g, 2 * m, 2)
 
         wait_group(term_in, t_recv, a, HALF - 1)
-        for o in (*order[::-1], 0):
+        for o in (*order, 0):
             t = hop(z, o, ZN)
             total = acc[pl.ds(pl.multiple_of(t * rows, rows), rows)] + chosen(a, HALF - 1, t, 1)
             zo_st[a, t] = total.astype(BF).reshape(RL, PT, 128)

time: 85.5 us -> 84.8 us (level)
  no operation moved by 1% of the time
where the time goes in v4:
time: 84.8 us; the launch traced here: 84.7 us
  Pallas kernels  84 us (99%)
    pallas_call x1, Pallas kernels, per_device(): pl.pallas_call(functools.partial(kernel, dims), out_shape=tuple((pltpu.VM...  83.2 us

profile of v4, /device:TPU:6, one launch (start us, length us, event | category | flops | bytes accessed | tf_op | source)
XLA Modules:
  0.0 84.7 jit_solution(15727859298494697306)
XLA Ops:
  0.6 83.2 %shard_map.102 = (bf16[128,1024]{1,0:T(8,128)(2,1)S(1)}, bf16[128,1024]{1,0:T(8,128)(2,1)S(1)}, bf16[2,2,16,128]{3,2,1,0:T(8,128)(2,1)S(1)}, bf16[2,2,16,128]{3,2,1,0:T(8,128)(2,1)S(1)}) custom-call(bf16[128,1024]{1,0:T(8,128)(2,1)} %x_hbm.1, bf16[128,1024]{1,0:T(8,128)(2,1)} %dy_hbm.1, bf16[2,2,128,128]{3,2,1,0:T(8,128)(2,1)} %wu_hbm.1, ...), custom_call_target="tpu_custom_call" | custom-call | flops 10000000000 | bytes 10000000 | tf_op jit(solution)/shard_map/pallas_call | solution.py:472
  83.8 0.8 shard_map.103

commit v5 on v4

--- a/solution.py
+++ b/solution.py
@@ -73,8 +73,7 @@
             ((x_hbm, x_ref), (dy_hbm, dy_ref), (wu_hbm, wu_ref), (wd_hbm, wd_ref), (keep_hbm, keep_ref))
         )
     ]
-    for one in fetch:
-        one.start()
+    fetch[0].start()
 
     order = [o for k in range(1, ZN // 2 + 1) for o in dict.fromkeys((k, ZN - k))]
     barrier = pltpu.get_barrier_semaphore()
@@ -87,18 +86,38 @@
         peers.append((hop(y, o, YN) * XC + xc, z))
     for b, t in peers:
         pl.semaphore_signal(barrier, inc=1, device_id=(b, t), device_id_type=MESH)
+    for one in fetch[1:]:
+        one.start()
 
     full = (full_x, full_dy)
     lane = iota((8, 128), 1)
     mine = jnp.where(lane == 0, rows_ref[0, 0], jnp.where(lane == 1, rows_ref[0, 1],
                      jnp.where(lane == 2, rows_ref[1, 0], rows_ref[1, 1])))
     rows_a[xc] = mine
-    for a, ref in enumerate((x_ref, dy_ref)):
+
+    def stage(a, ref):
         fetch[a].wait()
         for t in range(ZN):
             for i in range(RL):
                 zst[a, t, i] = ref[t * PT:(t + 1) * PT, i * 128:(i + 1) * 128]
         full[a][pl.ds(z * RL, RL)] = zst[a, z]
+
+    stage(0, x_ref)
+    pl.semaphore_wait(barrier, len(peers))
+
+    def row_a(o):
+        q = hop(xc, o, XC)
+        return remote(rows_a.at[xc], rows_a.at[xc], a_send.at[o], a_recv.at[xc], y * XC + q, z)
+
+    def z_copy(a, o):
+        t = hop(z, o, ZN)
+        return remote(zst.at[a, t], full[a].at[pl.ds(z * RL, RL)], z_send.at[a], z_recv.at[a], blk, t)
+
+    for o in order:
+        z_copy(0, o).start()
+    for o in range(1, XC):
+        row_a(o).start()
+    stage(1, dy_ref)
     fetch[2].wait()
     fetch[3].wait()
     for cl in range(2):
@@ -106,22 +125,6 @@
             live = s < cnt_ref[cl]
             wu[2 * up + cl, s * 128:(s + 1) * 128, :] = jnp.where(live, wu_ref[cl, s], jnp.zeros((), BF))
             wd[2 * up + cl, :, s * 128:(s + 1) * 128] = jnp.where(live, wd_ref[cl, s], jnp.zeros((), BF))
-    pl.semaphore_wait(barrier, len(peers))
-
-    def row_a(o):
-        q = hop(xc, o, XC)
-        return remote(rows_a.at[xc], rows_a.at[xc], a_send.at[o], a_recv.at[xc], y * XC + q, z)
-
-    for o in range(1, XC):
-        row_a(o).start()
-
-
-    def z_copy(a, o):
-        t = hop(z, o, ZN)
-        return remote(zst.at[a, t], full[a].at[pl.ds(z * RL, RL)], z_send.at[a], z_recv.at[a], blk, t)
-
-    for o in order:
-        z_copy(0, o).start()
 
     def w_slice(k, half, at):
         rows = (256, 128)[k] // ZN
@@ -385,14 +388,14 @@
         for s in range(ZN):
             for i in range(RL):
                 ref[s * PT:(s + 1) * PT, i * 128:(i + 1) * 128] = zo_in[a, s, i]
-
-    q_copy.wait_recv()
-    for cl in range(2):
-        own = gsum[2 * up + cl] + gpart[cl]
-        for s in range(2):
-            live = s < cnt_ref[cl]
-            for ref, k in ((gup_ref, 0), (gdn_ref, 1)):
-                ref[cl, s] = jnp.where(live, own[k, s], 0.0).astype(BF)
+        if a == 0:
+            q_copy.wait_recv()
+            for cl in range(2):
+                own = gsum[2 * up + cl] + gpart[cl]
+                for s in range(2):
+                    live = s < cnt_ref[cl]
+                    for ref, k in ((gup_ref, 0), (gdn_ref, 1)):
+                        ref[cl, s] = jnp.where(live, own[k, s], 0.0).astype(BF)
 
     for o in range(1, XC):
         row_a(o).wait_send()

time: 84.8 us -> 84.8 us (level)
  no operation moved by 1% of the time
where the time goes in v5:
time: 84.8 us; the launch traced here: 84.6 us
  Pallas kernels  84 us (99%)
    pallas_call x1, Pallas kernels, per_device(): pl.pallas_call(functools.partial(kernel, dims), out_shape=tuple((pltpu.VM...  83.2 us

profile of v5, /device:TPU:6, one launch (start us, length us, event | category | flops | bytes accessed | tf_op | source)
XLA Modules:
  0.0 84.6 jit_solution(17961902965735664233)
XLA Ops:
  0.6 83.2 %shard_map.102 = (bf16[128,1024]{1,0:T(8,128)(2,1)S(1)}, bf16[128,1024]{1,0:T(8,128)(2,1)S(1)}, bf16[2,2,16,128]{3,2,1,0:T(8,128)(2,1)S(1)}, bf16[2,2,16,128]{3,2,1,0:T(8,128)(2,1)S(1)}) custom-call(bf16[128,1024]{1,0:T(8,128)(2,1)} %x_hbm.1, bf16[128,1024]{1,0:T(8,128)(2,1)} %dy_hbm.1, bf16[2,2,128,128]{3,2,1,0:T(8,128)(2,1)} %wu_hbm.1, ...), custom_call_target="tpu_custom_call" | custom-call | flops 10000000000 | bytes 10000000 | tf_op jit(solution)/shard_map/pallas_call | solution.py:475
  83.8 0.8 shard_map.103
